TPU v7x, 32 devices: a whole 2x2x4 slice. The times are simulated.
32 devices in a mesh: fsdp: 16 (over z, x, core), tp: 2 (over y).
Axes of the slice: x: 2, y: 2, z: 4, core: 2. Of those that a mesh axis runs over, the one named last changes fastest.
Arguments:
- inputs: bfloat16 [32, 736, 1152], P('fsdp', 'tp'), may hold values from -6 to 6
- w_qkv: bfloat16 [3, 1152, 1152], P(None, 'fsdp', 'tp'), may hold values from -0.25 to 0.25
- w_out: bfloat16 [1152, 1152], P('tp', 'fsdp'), may hold values from -0.75 to 0.75
- w_up: bfloat16 [1152, 4304], P('fsdp', 'tp'), may hold values from -0.1875 to 0.1875
- w_down: bfloat16 [4304, 1152], P('tp', 'fsdp'), may hold values from -0.09375 to 0.09375
- norm_gains: float32 [2, 1152], replicated, may hold values from 0.1 to 1.9
- biases: float32 [6, 1152], replicated, may hold values from -3 to 3
- up_bias: float32 [4304], replicated, may hold values from -3 to 3
- cotangent: bfloat16 [32, 736, 1152], P('fsdp', 'tp'), may hold values from -6 to 6
Outputs:
- outputs: bfloat16 [32, 736, 1152], P('fsdp', 'tp')
- input_grad: float32 [32, 736, 1152], P('fsdp', 'tp')
- w_qkv_grad: float32 [3, 1152, 1152], P(None, 'fsdp', 'tp')
- w_out_grad: float32 [1152, 1152], P('tp', 'fsdp')
- w_up_grad: float32 [1152, 4304], P('fsdp', 'tp')
- w_down_grad: float32 [4304, 1152], P('tp', 'fsdp')
- norm_gains_grad: float32 [2, 1152], replicated
- biases_grad: float32 [6, 1152], replicated
- up_bias_grad: float32 [4304], replicated
All inputs are finite; a program needn't handle non-finite values.
Results may differ from a plain program's by a relative error of at most 0.018.
The roundings to bfloat16 on the way count: a program that leaves them out, or rounds other values in their place, can miss the bound.
Values may be sent and summed in bfloat16 or wider, within the bound.
A program may use at most 192 MiB of HBM per device.

v0:
```python
import math
import jax
import jax.numpy as jnp
from jax import lax
from jax.sharding import PartitionSpec as P

HD = 72
VALID = 729
norm_eps = 1e-06
gelu_coef = math.sqrt(2.0 / math.pi)


def norm_forward(values, scale_row, shift_row):
    average = jnp.mean(values, axis=-1, keepdims=True)
    centred = values - average
    inv_std = lax.rsqrt(jnp.mean(centred * centred, axis=-1, keepdims=True) + norm_eps)
    normed = centred * inv_std
    return (normed * scale_row + shift_row, normed, inv_std)


def norm_backward(upstream, normed, inv_std, scale_row):
    scaled = upstream * scale_row
    back = inv_std * (
        scaled
        - jnp.mean(scaled, axis=-1, keepdims=True)
        - normed * jnp.mean(scaled * normed, axis=-1, keepdims=True)
    )
    return (back, jnp.sum(upstream * normed, axis=0), jnp.sum(upstream, axis=0))


def gelu_tanh(pre_act):
    return (
        0.5
        * pre_act
        * (1.0 + jnp.tanh(gelu_coef * (pre_act + 0.044715 * pre_act * pre_act * pre_act)))
    )


def gelu_slope(pre_act):
    tangent = jnp.tanh(gelu_coef * (pre_act + 0.044715 * pre_act * pre_act * pre_act))
    inner_slope = gelu_coef * (1.0 + 3.0 * 0.044715 * pre_act * pre_act)
    return 0.5 * (1.0 + tangent) + 0.5 * pre_act * (1.0 - tangent * tangent) * inner_slope


def masked_scores(queries, key_rows, positions):
    seq_len = queries.shape[0]
    head_count = queries.shape[1] // HD
    query_heads = queries.reshape(seq_len, head_count, HD)
    key_heads = key_rows.reshape(seq_len, head_count, HD)
    scores = jnp.einsum("qhe,khe->hqk", query_heads, key_heads, preferred_element_type=jnp.float32)
    scores = scores * (1.0 / math.sqrt(HD))
    visible = (positions < VALID)[None, None, :]
    return (jnp.where(visible, scores, -1e30), query_heads, key_heads)


def attend_forward(queries, key_rows, values, positions):
    seq_len = queries.shape[0]
    scores, query_heads, key_heads = masked_scores(queries, key_rows, positions)
    value_heads = values.reshape(seq_len, -1, HD)
    largest = jnp.max(scores, axis=-1, keepdims=True)
    powers = jnp.exp(scores - largest)
    summed = jnp.sum(powers, axis=-1, keepdims=True)
    attn_probs = (powers / summed).astype(jnp.bfloat16)
    mixed_out = jnp.einsum(
        "hqk,khe->qhe", attn_probs, value_heads, preferred_element_type=jnp.float32
    )
    log_totals = (largest + jnp.log(summed))[:, :, 0]
    return (mixed_out.reshape(seq_len, queries.shape[1]).astype(jnp.bfloat16), log_totals)


def attend_backward(queries, key_rows, values, log_totals, d_mixed, positions):
    seq_len = queries.shape[0]
    scores, query_heads, key_heads = masked_scores(queries, key_rows, positions)
    value_heads = values.reshape(seq_len, -1, HD)
    grad_heads = d_mixed.reshape(seq_len, -1, HD)
    probs_full = jnp.exp(scores - log_totals[:, :, None])
    d_probs = jnp.einsum(
        "qhe,khe->hqk", grad_heads, value_heads, preferred_element_type=jnp.float32
    )
    row_inner = jnp.sum(probs_full * d_probs, axis=-1, keepdims=True)
    d_scores = (probs_full * (d_probs - row_inner)).astype(jnp.bfloat16)
    d_values = jnp.einsum(
        "hqk,qhe->khe",
        probs_full.astype(jnp.bfloat16),
        grad_heads,
        preferred_element_type=jnp.float32,
    )
    scale_now = 1.0 / math.sqrt(HD)
    d_queries = (
        jnp.einsum("hqk,khe->qhe", d_scores, key_heads, preferred_element_type=jnp.float32)
        * scale_now
    )
    d_keys = (
        jnp.einsum("hqk,qhe->khe", d_scores, query_heads, preferred_element_type=jnp.float32)
        * scale_now
    )
    parts = [d_queries, d_keys, d_values]
    return jnp.concatenate(
        [part.reshape(seq_len, queries.shape[1]).astype(jnp.bfloat16) for part in parts], axis=1
    )


def dot(left, right, dims):
    return lax.dot_general(left, right, (dims, ((), ())), preferred_element_type=jnp.float32)


ROWS_COLS = ((1,), (0,))
ROWS_ROWS = ((1,), (1,))
COLS_COLS = ((0,), (0,))


def swap_halves(block):
    return lax.ppermute(block, "tp", [(0, 1), (1, 0)])


def gather_rows(block):
    if lax.axis_size("tp") == 2:
        return jnp.concatenate([block, swap_halves(block)], axis=0)
    return lax.all_gather(block, "tp", axis=0, tiled=True)


def scatter_dot(left, right, dims):
    if lax.axis_size("tp") == 2:
        half = left.shape[0] // 2
        away = swap_halves(dot(left[half:], right, dims).astype(jnp.bfloat16))
        return dot(left[:half], right, dims) + away.astype(jnp.float32)
    return lax.psum_scatter(
        dot(left, right, dims).astype(jnp.bfloat16), "tp", scatter_dimension=0, tiled=True
    ).astype(jnp.float32)


def gather_weight(shard):
    return lax.all_gather(shard, "fsdp", axis=0, tiled=True)


def scatter_weight(whole):
    return lax.psum_scatter(
        whole.astype(jnp.bfloat16), "fsdp", scatter_dimension=0, tiled=True
    ).astype(jnp.float32)


def per_device(inputs, w_qkv, w_out, w_up, w_down, norm_gains, biases, up_bias, cotangent):
    image_count, rows_here, width = inputs.shape
    images = range(image_count)
    local_cols = w_qkv.shape[2]
    unit_count = w_up.shape[1]
    shard_rows = w_qkv.shape[1]
    tp_index = lax.axis_index("tp")
    seq_len = rows_here * lax.axis_size("tp")
    col_start = tp_index * local_cols
    unit_start = tp_index * unit_count
    positions = lax.iota(jnp.int32, seq_len)
    if lax.axis_size("tp") == 2:
        positions = positions + tp_index * rows_here
        positions = jnp.where(positions >= seq_len, positions - seq_len, positions)
    qkv_all = gather_weight(w_qkv.transpose(1, 0, 2).reshape(shard_rows, 3 * local_cols))
    out_all = gather_weight(w_out.T)
    up_all = gather_weight(w_up)
    down_all = gather_weight(w_down.T)
    query_bias = lax.dynamic_slice_in_dim(biases[1], col_start, local_cols)
    value_bias = lax.dynamic_slice_in_dim(biases[2], col_start, local_cols)
    unit_bias = lax.dynamic_slice_in_dim(up_bias, unit_start, unit_count)
    qkv_bias = jnp.concatenate([query_bias, jnp.zeros_like(query_bias), value_bias])
    residual = [inputs[i].astype(jnp.float32) for i in images]
    first = [norm_forward(residual[i], norm_gains[0], biases[0]) for i in images]
    gathered_one = [gather_rows(first[i][0].astype(jnp.bfloat16)) for i in images]
    grad_rows = [gather_rows(cotangent[i]) for i in images]
    saved, mixed, middle, second, gathered_two = ([], [], [], [], [])
    for i in images:
        projected = (dot(gathered_one[i], qkv_all, ROWS_COLS) + qkv_bias).astype(jnp.bfloat16)
        queries, key_rows, values = (
            projected[:, c * local_cols : (c + 1) * local_cols] for c in range(3)
        )
        mixed_out, log_totals = attend_forward(queries, key_rows, values, positions)
        saved.append((queries, key_rows, values, log_totals))
        mixed.append(mixed_out)
        middle.append(residual[i] + scatter_dot(mixed_out, out_all, ROWS_ROWS) + biases[3])
        second.append(norm_forward(middle[i], norm_gains[1], biases[4]))
        gathered_two.append(gather_rows(second[i][0].astype(jnp.bfloat16)))
    activated, d_pre, outputs, d_normed_two = ([], [], [], [])
    for i in images:
        pre_act = dot(gathered_two[i], up_all, ROWS_COLS) + unit_bias
        activated.append(gelu_tanh(pre_act).astype(jnp.bfloat16))
        d_act = dot(grad_rows[i], down_all, ROWS_COLS)
        d_pre.append((d_act * gelu_slope(pre_act)).astype(jnp.bfloat16))
        d_normed_two.append(scatter_dot(d_pre[i], up_all, ROWS_ROWS))
        mlp_rows = scatter_dot(activated[i], down_all, ROWS_ROWS)
        outputs.append((middle[i] + mlp_rows + biases[5]).astype(jnp.bfloat16))

    def joined(parts):
        return jnp.concatenate(parts, axis=0)

    grads_whole, units_whole = (joined(grad_rows), joined(d_pre))
    down_grad = scatter_weight(dot(grads_whole, joined(activated), COLS_COLS)).T
    up_grad = scatter_weight(dot(joined(gathered_two), units_whole, COLS_COLS))
    unit_sums = jnp.sum(units_whole, axis=0, dtype=jnp.float32)
    gain_two, shift_two, d_middle, branch = ([], [], [], [])
    for i in images:
        back, gain_part, shift_part = norm_backward(
            d_normed_two[i], second[i][1], second[i][2], norm_gains[1]
        )
        gain_two.append(gain_part)
        shift_two.append(shift_part)
        d_middle.append(cotangent[i].astype(jnp.float32) + back)
        branch.append(gather_rows(d_middle[i].astype(jnp.bfloat16)))
    d_qkv, d_normed_one = ([], [])
    for i in images:
        d_mixed = dot(branch[i], out_all, ROWS_COLS).astype(jnp.bfloat16)
        d_qkv.append(attend_backward(*saved[i], d_mixed, positions))
        d_normed_one.append(scatter_dot(d_qkv[i], qkv_all, ROWS_ROWS))
    out_grad = scatter_weight(dot(joined(branch), joined(mixed), COLS_COLS)).T
    qkv_whole = joined(d_qkv)
    qkv_grad = scatter_weight(dot(joined(gathered_one), qkv_whole, COLS_COLS))
    qkv_grad = qkv_grad.reshape(shard_rows, 3, local_cols).transpose(1, 0, 2)
    qkv_sums = jnp.sum(qkv_whole, axis=0, dtype=jnp.float32)
    input_grad, gain_one, shift_one = ([], [], [])
    for i in images:
        back, gain_part, shift_part = norm_backward(
            d_normed_one[i], first[i][1], first[i][2], norm_gains[0]
        )
        gain_one.append(gain_part)
        shift_one.append(shift_part)
        input_grad.append(d_middle[i] + back)
    blank_row = jnp.zeros((width,), jnp.float32)
    query_sums = lax.dynamic_update_slice_in_dim(blank_row, qkv_sums[:local_cols], col_start, 0)
    value_sums = lax.dynamic_update_slice_in_dim(
        blank_row, qkv_sums[2 * local_cols :], col_start, 0
    )
    unit_row = lax.dynamic_update_slice_in_dim(jnp.zeros_like(up_bias), unit_sums, unit_start, 0)
    out_sums = sum((jnp.sum(d_middle[i], axis=0) for i in images))
    top_sums = jnp.sum(cotangent, axis=(0, 1), dtype=jnp.float32)
    pieces = [
        sum(gain_one),
        sum(shift_one),
        query_sums,
        value_sums,
        sum(gain_two),
        sum(shift_two),
        out_sums,
        top_sums,
        unit_row,
    ]
    total = lax.psum(jnp.concatenate(pieces), ("fsdp", "tp"))
    rows = total[: 8 * width].reshape(8, width)
    gain_total = jnp.stack([rows[0], rows[4]])
    bias_total = jnp.stack([rows[1], rows[2], rows[3], rows[6], rows[5], rows[7]])
    return (
        jnp.stack(outputs),
        jnp.stack(input_grad),
        qkv_grad,
        out_grad,
        up_grad,
        down_grad,
        gain_total,
        bias_total,
        total[8 * width :],
    )


def solution(mesh):
    return jax.shard_map(
        per_device,
        mesh=mesh,
        in_specs=(
            P("fsdp", "tp", None),
            P(None, "fsdp", "tp"),
            P("tp", "fsdp"),
            P("fsdp", "tp"),
            P("tp", "fsdp"),
            P(),
            P(),
            P(),
            P("fsdp", "tp", None),
        ),
        out_specs=(
            P("fsdp", "tp", None),
            P("fsdp", "tp", None),
            P(None, "fsdp", "tp"),
            P("tp", "fsdp"),
            P("fsdp", "tp"),
            P("tp", "fsdp"),
            P(),
            P(),
            P(),
        ),
        check_vma=False,
    )
```

profile of v0, /device:TPU:0, one launch (start us, length us, event | category | flops | bytes accessed | tf_op | source)
XLA Modules:
  0.0 649.6 jit_solution(3423712494130585117)
XLA Ops:
  15.5 3.0 collective-permute-start.4
  18.9 19.4 %collective-permute-done.4 = bf16[368,1152]{1,0:T(8,128)(2,1)} collective-permute-done((bf16[368,1152]{1,0:T(8,128)(2,1)S(1)}, bf16[368,1152]{1,0:T(8,128)(2,1)}, u32[]{:S(2)}, u32[]{:S(2)}) %collective-permute-start.4) | collective-permute-done | bytes 847904 | tf_op jit(solution)/shard_map/ppermute | solution.py:113
  38.4 25.5 %all-gather.5.cloned.1.call-done = bf16[1152,1728]{1,0:T(8,128)(2,1)} async-done(((bf16[72,1728]{1,0:T(8,128)(2,1)}), bf16[1152,1728]{1,0:T(8,128)(2,1)}) %all-gather.5.cloned.1.call-update) | async-done | bytes 3981328 | tf_op jit(solution)/shard_map/all_gather | solution.py:133
  63.9 6.0 add_convert_fusion
  78.6 6.0 add_convert_fusion.1
  93.1 9.6 %fusion.204 = (f32[8,736]{1,0:T(8,128)S(1)}, f32[8,736,736]{1,2,0:T(8,128)}) fusion(bf16[736,8,72]{0,2,1:T(8,128)(2,1)} %bitcast.205, bf16[736,8,72]{0,2,1:T(8,128)(2,1)S(1)} %bitcast.195, pred[736]{0:T(1024)(128)(4,1)S(1)} %fusion.180), kind=kOutput, calls=%fused_computation.287 | convolution fusion | flops 637028608 | bytes 19054304 | tf_op jit(solution)/shard_map/qhe,khe->hqk/dot_general | solution.py:50
  102.6 8.8 %fusion = f32[8,736]{1,0:T(8,128)S(1)} fusion(f32[8,736,736]{1,2,0:T(8,128)} %get-tuple-element.102, f32[8,736]{1,0:T(8,128)S(1)} %get-tuple-element.101), kind=kLoop, calls=%fused_computation.12 | loop fusion | flops 8661248 | bytes 17381376 | tf_op jit(solution)/shard_map/reduce_sum | solution.py:62
  111.4 8.9 %fusion.157 = bf16[8,72,736]{2,1,0:T(8,128)(2,1)S(1)} fusion(bf16[736,8,72]{0,2,1:T(8,128)(2,1)S(1)} %bitcast.215, f32[8,736,736]{1,2,0:T(8,128)} %get-tuple-element.102, f32[8,736]{1,0:T(8,128)S(1)} %fusion, f32[8,736]{1,0:T(8,128)S(1)} %get-tuple-element.101), kind=kOutput, calls=%fused_computation.211 | convolution fusion | flops 637458432 | bytes 19077120 | tf_op jit(solution)/shard_map/hqk,khe->qhe/dot_general | solution.py:64
  122.4 3.4 convolution_convert_fusion.10
  127.3 9.2 %fusion.205 = (f32[8,736]{1,0:T(8,128)S(1)}, f32[8,736,736]{1,2,0:T(8,128)}) fusion(bf16[736,8,72]{0,2,1:T(8,128)(2,1)S(1)} %bitcast.207, bf16[736,8,72]{0,2,1:T(8,128)(2,1)S(1)} %bitcast.197, pred[736]{0:T(1024)(128)(4,1)} %copy-done.72), kind=kOutput, calls=%fused_computation.288 | convolution fusion | flops 637028608 | bytes 19054304 | tf_op jit(solution)/shard_map/qhe,khe->hqk/dot_general | solution.py:50
  136.5 8.8 %fusion.1 = f32[8,736]{1,0:T(8,128)S(1)} fusion(f32[8,736,736]{1,2,0:T(8,128)} %get-tuple-element.104, f32[8,736]{1,0:T(8,128)S(1)} %get-tuple-element.103), kind=kLoop, calls=%fused_computation.13 | loop fusion | flops 8661248 | bytes 17381376 | tf_op jit(solution)/shard_map/reduce_sum | solution.py:62
  145.4 8.6 %fusion.156 = bf16[8,72,736]{2,1,0:T(8,128)(2,1)S(1)} fusion(bf16[736,8,72]{0,2,1:T(8,128)(2,1)S(1)} %bitcast.217, f32[8,736,736]{1,2,0:T(8,128)} %get-tuple-element.104, f32[8,736]{1,0:T(8,128)S(1)} %fusion.1, f32[8,736]{1,0:T(8,128)S(1)} %get-tuple-element.103), kind=kOutput, calls=%fused_computation.210 | convolution fusion | flops 637458432 | bytes 19077120 | tf_op jit(solution)/shard_map/hqk,khe->qhe/dot_general | solution.py:64
  156.8 19.2 %collective-permute-done.5 = bf16[368,1152]{1,0:T(8,128)(2,1)S(1)} collective-permute-done((bf16[368,1152]{1,0:T(8,128)(2,1)S(1)}, bf16[368,1152]{1,0:T(8,128)(2,1)S(1)}, u32[]{:S(2)}, u32[]{:S(2)}) %collective-permute-start.5) | collective-permute-done | bytes 847904 | tf_op jit(solution)/shard_map/ppermute | solution.py:113
  185.5 17.8 %collective-permute-done.6 = bf16[368,1152]{1,0:T(8,128)(2,1)} collective-permute-done((bf16[368,1152]{1,0:T(8,128)(2,1)}, bf16[368,1152]{1,0:T(8,128)(2,1)}, u32[]{:S(2)}, u32[]{:S(2)}) %collective-permute-start.6) | collective-permute-done | bytes 847904 | tf_op jit(solution)/shard_map/ppermute | solution.py:113
  203.3 10.3 %fusion.112 = f32[736,2152]{1,0:T(8,128)} fusion(bf16[1152,2152]{1,0:T(8,128)(2,1)} %all-gather.9.cloned.1.call-done, bf16[368,1152]{1,0:T(8,128)(2,1)} %collective-permute-done.6, bf16[368,1152]{1,0:T(8,128)(2,1)} %get-tuple-element.94), kind=kOutput, calls=%fused_computation.155 | convolution fusion | flops 3652632576 | bytes 12989440 | tf_op jit(solution)/shard_map/dot_general | solution.py:104
  213.6 26.0 %collective-permute-done.12 = bf16[368,1152]{1,0:T(8,128)(2,1)} collective-permute-done((bf16[368,1152]{1,0:T(8,128)(2,1)S(1)}, bf16[368,1152]{1,0:T(8,128)(2,1)}, u32[]{:S(2)}, u32[]{:S(2)}) %collective-permute-start.12) | collective-permute-done | bytes 847904 | tf_op jit(solution)/shard_map/ppermute | solution.py:113
  239.6 11.1 %fusion.27 = bf16[736,2152]{1,0:T(8,128)(2,1)S(1)} fusion(bf16[1152,2152]{1,0:T(8,128)(2,1)} %all-gather.11.cloned.1.call-done, f32[736,2152]{1,0:T(8,128)} %fusion.112, f32[2152]{0:T(1024)S(1)} %dynamic_slice.17, bf16[368,1152]{1,0:T(8,128)(2,1)} %collective-permute-done.12, bf16[368,1152]{1,0:T(8,128)(2,1)S(1)} %get-tuple-element.78), kind=kOutput, calls=%fused_computation.46 | convolution fusion | flops 3684310016 | bytes 16165792 | tf_op jit(solution)/shard_map/dot_general | solution.py:104
  253.8 4.0 collective-permute-done.2
  257.8 11.5 %multiply_convert_fusion.3 = (bf16[736,2152]{1,0:T(8,128)(2,1)}, bf16[736,2152]{1,0:T(8,128)(2,1)}, f32[736,2152]{1,0:T(8,128)}) fusion(f32[2152]{0:T(1024)S(1)} %dynamic_slice.17, f32[736,2152]{1,0:T(8,128)} %fusion.112, bf16[1152,2152]{1,0:T(8,128)(2,1)S(1)} %copy-done.73, bf16[368,1152]{1,0:T(8,128)(2,1)} %collective-permute-done.2, ...), kind=kOutput, calls=%fused_computation.52 | convolution fusion | flops 3684310016 | bytes 25669024 | tf_op jit(solution)/shard_map/dot_general | solution.py:104
  269.3 9.6 %fusion.21 = bf16[736,2152]{1,0:T(8,128)(2,1)S(1)} fusion(bf16[1152,2152]{1,0:T(8,128)(2,1)S(1)} %bitcast.236, f32[736,2152]{1,0:T(8,128)} %get-tuple-element.105, f32[2152]{0:T(1024)S(1)} %dynamic_slice.17, bf16[368,1152]{1,0:T(8,128)(2,1)} %collective-permute-done.8, bf16[368,1152]{1,0:T(8,128)(2,1)S(1)} %get-tuple-element.77), kind=kOutput, calls=%fused_computation.40 | convolution fusion | flops 3684310016 | bytes 16165792 | tf_op jit(solution)/shard_map/dot_general | solution.py:104
  284.4 14.1 %collective-permute-done.9 = bf16[368,1152]{1,0:T(8,128)(2,1)S(1)} collective-permute-done((bf16[368,1152]{1,0:T(8,128)(2,1)S(1)}, bf16[368,1152]{1,0:T(8,128)(2,1)S(1)}, u32[]{:S(2)}, u32[]{:S(2)}) %collective-permute-start.9) | collective-permute-done | bytes 847904 | tf_op jit(solution)/shard_map/ppermute | solution.py:113
  298.6 3.7 multiply_reduce_fusion.3
  308.4 19.8 %collective-permute-done.14 = bf16[368,1152]{1,0:T(8,128)(2,1)S(1)} collective-permute-done((bf16[368,1152]{1,0:T(8,128)(2,1)S(1)}, bf16[368,1152]{1,0:T(8,128)(2,1)S(1)}, u32[]{:S(2)}, u32[]{:S(2)}) %collective-permute-start.14) | collective-permute-done | bytes 847904 | tf_op jit(solution)/shard_map/ppermute | solution.py:113
  328.2 12.6 %collective-permute-done.10 = bf16[368,1152]{1,0:T(8,128)(2,1)S(1)} collective-permute-done((bf16[368,1152]{1,0:T(8,128)(2,1)S(1)}, bf16[368,1152]{1,0:T(8,128)(2,1)S(1)}, u32[]{:S(2)}, u32[]{:S(2)}) %collective-permute-start.10) | collective-permute-done | bytes 847904 | tf_op jit(solution)/shard_map/ppermute | solution.py:113
  341.7 4.7 fusion.60
  346.4 14.3 %convolution_convert_fusion.1 = bf16[1152,2152]{1,0:T(8,128)(2,1)} fusion(bf16[736,2152]{1,0:T(8,128)(2,1)} %copy-done.24, bf16[736,2152]{1,0:T(8,128)(2,1)} %copy-done.25, bf16[368,1152]{1,0:T(8,128)(2,1)} %collective-permute-done.6, bf16[368,1152]{1,0:T(8,128)(2,1)} %get-tuple-element.94, bf16[368,1152]{1,0:T(8,128)(2,1)} %collective-permute-done.2, ...), kind=kOutput, calls=%fused_computation.18 | convolution fusion | flops 7327198208 | bytes 14685184 | tf_op jit(solution)/shard_map/dot_general | solution.py:104
  363.2 6.3 convolution_convert_fusion.7
  370.7 6.0 convolution_convert_fusion.9
  377.7 13.0 %convolution_convert_fusion = bf16[1152,2152]{1,0:T(8,128)(2,1)} fusion(bf16[736,2152]{1,0:T(8,128)(2,1)S(1)} %copy-done.83, bf16[736,2152]{1,0:T(8,128)(2,1)S(1)} %copy-done.81, bf16[368,1152]{1,0:T(8,128)(2,1)} %collective-permute-done.12, bf16[368,1152]{1,0:T(8,128)(2,1)S(1)} %copy-done.38, bf16[368,1152]{1,0:T(8,128)(2,1)} %collective-permute-done.8, ...), kind=kOutput, calls=%fused_computation.17 | convolution fusion | flops 7327198208 | bytes 14685184 | tf_op jit(solution)/shard_map/dot_general | solution.py:104
  390.6 3.9 convert_reduce_fusion
  395.4 5.7 fusion.145
  403.5 5.1 fusion.153
  412.5 10.2 %fusion.161 = bf16[8,72,736]{2,1,0:T(8,128)(2,1)S(1)} fusion(bf16[736,8,72]{0,2,1:T(8,128)(2,1)S(1)} %bitcast.221, f32[8,736,736]{1,2,0:T(8,128)} %get-tuple-element.104, f32[8,736]{1,0:T(8,128)S(1)} %log_add_fusion), kind=kOutput, calls=%fused_computation.213 | convolution fusion | flops 633124864 | bytes 19053568 | tf_op jit(solution)/shard_map/hqk,qhe->khe/dot_general | solution.py:82
  422.7 12.4 %multiply_reduce_fusion = (f32[8,736]{1,0:T(8,128)S(1)}, f32[8,736,736]{1,2,0:T(8,128)}) fusion(f32[8,736,736]{1,2,0:T(8,128)} %get-tuple-element.104, f32[8,736]{1,0:T(8,128)S(1)} %log_add_fusion, bf16[736,8,72]{0,2,1:T(8,128)(2,1)S(1)} %bitcast.222, bf16[736,8,72]{0,2,1:T(8,128)(2,1)S(1)} %bitcast.218), kind=kOutput, calls=%fused_computation.1 | convolution fusion | flops 637028608 | bytes 36411392 | tf_op jit(solution)/shard_map/qhe,khe->hqk/dot_general | solution.py:77
  435.0 12.9 %multiply_convert_fusion = bf16[8,736,736]{1,2,0:T(8,128)(2,1)S(1)} fusion(f32[8,736,736]{1,2,0:T(8,128)} %get-tuple-element.110, f32[8,736,736]{1,2,0:T(8,128)} %get-tuple-element.104, f32[8,736]{1,0:T(8,128)S(1)} %get-tuple-element.109, f32[8,736]{1,0:T(8,128)S(1)} %log_add_fusion), kind=kLoop, calls=%fused_computation | loop fusion | flops 17334272 | bytes 43382784 | tf_op jit(solution)/shard_map/convert_element_type | solution.py:81
  454.7 3.4 convolution_convert_fusion.3
  461.1 11.6 %multiply_reduce_fusion.1 = (f32[8,736]{1,0:T(8,128)S(1)}, f32[8,736,736]{1,2,0:T(8,128)}) fusion(f32[8,736,736]{1,2,0:T(8,128)} %get-tuple-element.102, f32[8,736]{1,0:T(8,128)S(1)} %log_add_fusion.1, bf16[736,8,72]{0,2,1:T(8,128)(2,1)S(1)} %bitcast.219, bf16[736,8,72]{0,2,1:T(8,128)(2,1)S(1)} %bitcast.216), kind=kOutput, calls=%fused_computation.4 | convolution fusion | flops 637028608 | bytes 36411392 | tf_op jit(solution)/shard_map/qhe,khe->hqk/dot_general | solution.py:77
  472.7 13.0 %multiply_convert_fusion.1 = bf16[8,736,736]{1,2,0:T(8,128)(2,1)S(1)} fusion(f32[8,736,736]{1,2,0:T(8,128)} %get-tuple-element.108, f32[8,736,736]{1,2,0:T(8,128)} %get-tuple-element.102, f32[8,736]{1,0:T(8,128)S(1)} %get-tuple-element.107, f32[8,736]{1,0:T(8,128)S(1)} %log_add_fusion.1), kind=kLoop, calls=%fused_computation.3 | loop fusion | flops 17334272 | bytes 43382784 | tf_op jit(solution)/shard_map/convert_element_type | solution.py:81
  485.7 2.8 multiply_convert_fusion.6
  490.2 9.5 %fusion.158 = bf16[8,72,736]{2,1,0:T(8,128)(2,1)S(1)} fusion(bf16[736,8,72]{0,2,1:T(8,128)(2,1)S(1)} %bitcast.220, f32[8,736,736]{1,2,0:T(8,128)} %get-tuple-element.102, f32[8,736]{1,0:T(8,128)S(1)} %copy-done.47), kind=kOutput, calls=%fused_computation.212 | convolution fusion | flops 633124864 | bytes 19053568 | tf_op jit(solution)/shard_map/hqk,qhe->khe/dot_general | solution.py:82
  502.5 3.4 convolution_convert_fusion.4
  506.1 12.6 %convolution_convert_fusion.2 = bf16[1152,1728]{1,0:T(8,128)(2,1)} fusion(bf16[368,1152]{1,0:T(8,128)(2,1)} %collective-permute-done.4, bf16[368,1152]{1,0:T(8,128)(2,1)} %copy-done.45, bf16[368,1152]{1,0:T(8,128)(2,1)} %collective-permute-done, bf16[368,1152]{1,0:T(8,128)(2,1)} %copy-done.44, bf16[736,576]{0,1:T(8,128)(2,1)S(1)} %bitcast.210, ...), kind=kOutput, calls=%fused_computation.30 | convolution fusion | flops 5906571264 | bytes 12460032 | tf_op jit(solution)/shard_map/dot_general | solution.py:104
  518.7 13.3 %convert_reduce_fusion.1 = f32[1728]{0:T(1024)S(1)} fusion(bf16[736,576]{0,1:T(8,128)(2,1)} %bitcast.211, bf16[736,576]{0,1:T(8,128)(2,1)S(1)} %bitcast.201, bf16[736,576]{0,1:T(8,128)(2,1)S(1)} %bitcast.191, bf16[736,576]{0,1:T(8,128)(2,1)} %bitcast.214, bf16[736,576]{0,1:T(8,128)(2,1)S(1)} %bitcast.204, bf16[736,576]{0,1:T(8,128)(2,1)S(1)} %bitcast.194), kind=kLoop, calls=%fused_computation.19 | loop fusion | flops 33065280 | bytes 5094144 | tf_op jit(solution)/shard_map/reduce_sum | solution.py:215
  532.5 5.2 convert_add_fusion
  538.1 6.9 %fusion.98 = (f32[1152]{0:T(1024)S(1)}, f32[368]{0:T(512)}, f32[368]{0:T(512)}, f32[1152]{0:T(1024)S(1)}, f32[368]{0:T(512)S(1)}, /*index=5*/f32[368]{0:T(512)S(...) fusion(f32[368]{0:T(512)S(1)} %copy-done.63, f32[368]{0:T(512)S(1)} %copy-done.57, ...), kind=kOutput, calls=%fused_computation.141 | convolution fusion | flops 1474443264 | bytes 11431680 | tf_op jit(solution)/shard_map/dot_general | solution.py:104
  545.1 40.5 %psum.7 = f32[13520]{0:T(1024)S(1)} all-reduce(f32[13520]{0:T(1024)S(1)} %constant_dynamic-update-slice_fusion), channel_id=1, replica_groups=mesh['fsdp'=16,'tp'=2] {'fsdp','tp'}, use_global_device_ids=true, to_apply=%region_39.40 | all-reduce | flops 13520 | bytes 108160 | tf_op jit(solution)/shard_map/psum | solution.py:243
  589.0 3.1 fusion.97
  599.3 41.2 %reduce-scatter.11.cloned.1.call-done = bf16[72,1728]{1,0:T(8,128)(2,1)} async-done(((bf16[1152,1728]{1,0:T(8,128)(2,1)}), bf16[72,1728]{1,0:T(8,128)(2,1)}) %reduce-scatter.11.cloned.1.call-update) | async-done | bytes 248848 | tf_op jit(solution)/shard_map/reduce_scatter | solution.py:137
  (313 shorter events, 96.2 us)
Async XLA Ops:
  7.2 56.7 %all-gather.5.cloned.1.call-start = ((), (), s32[]{:S(2)}) async-start(), calls=%async_computation.4 | async-start | bytes 4386816 | tf_op jit(solution)/shard_map/all_gather | solution.py:133
  9.4 112.9 %all-gather.7.cloned.1.call-start = ((), (), s32[]{:S(2)}) async-start(), calls=%async_computation.5 | async-start | bytes 1566720 | tf_op jit(solution)/shard_map/all_gather | solution.py:133
  10.2 193.1 %all-gather.9.cloned.1.call-start = ((), (), s32[]{:S(2)}) async-start(), calls=%async_computation.6 | async-start | bytes 5326848 | tf_op jit(solution)/shard_map/all_gather | solution.py:133
  10.9 228.7 %all-gather.11.cloned.1.call-start = ((), (), s32[]{:S(2)}) async-start(), calls=%async_computation.7 | async-start | bytes 5326848 | tf_op jit(solution)/shard_map/all_gather | solution.py:133
  13.5 56.4 %copy-start.54 = (f32[368]{0:T(512)}, f32[368]{0:T(512)S(1)}, u32[]{:S(2)}) copy-start(f32[368]{0:T(512)S(1)} %get-tuple-element.114) | copy-start | bytes 4420
  13.5 56.4 %copy-start.56 = (f32[368]{0:T(512)}, f32[368]{0:T(512)S(1)}, u32[]{:S(2)}) copy-start(f32[368]{0:T(512)S(1)} %get-tuple-element.115) | copy-start | bytes 4420
  14.1 55.8 %copy-start.62 = (f32[368]{0:T(512)}, f32[368]{0:T(512)S(1)}, u32[]{:S(2)}) copy-start(f32[368]{0:T(512)S(1)} %add_rsqrt_fusion.3) | copy-start | bytes 4420
  14.2 55.8 %copy-start.64 = (f32[368]{0:T(512)}, f32[368]{0:T(512)S(1)}, u32[]{:S(2)}) copy-start(f32[368]{0:T(512)S(1)} %add_rsqrt_fusion.1) | copy-start | bytes 4420
  15.5 54.4 %copy-start.45 = (bf16[368,1152]{1,0:T(8,128)(2,1)}, bf16[368,1152]{1,0:T(8,128)(2,1)S(1)}, u32[]{:S(2)}) copy-start(bf16[368,1152]{1,0:T(8,128)(2,1)S(1)} %get-tuple-element.70) | copy-start | bytes 2543620
  15.5 63.1 %copy-start.44 = (bf16[368,1152]{1,0:T(8,128)(2,1)}, bf16[368,1152]{1,0:T(8,128)(2,1)S(1)}, u32[]{:S(2)}) copy-start(bf16[368,1152]{1,0:T(8,128)(2,1)S(1)} %get-tuple-element.69) | copy-start | bytes 2543620
  15.5 22.8 %collective-permute-start.4 = (bf16[368,1152]{1,0:T(8,128)(2,1)S(1)}, bf16[368,1152]{1,0:T(8,128)(2,1)}, u32[]{:S(2)}, u32[]{:S(2)}) collective-permute-start(bf16[368,1152]{1,0:T(8,128)(2,1)S(1)} %get-tuple-element.70), channel_id=1, source_target_pairs={{0,1},{1,0},{2,3},{3,2},{4,5},{5,4},{6,7},{7,6},{8,9},{9,8},{10,11... | collective-permute-start | bytes 2543624 | tf_op jit(solution)/shard_map/ppermute | solution.py:113
  18.6 60.0 %collective-permute-start = (bf16[368,1152]{1,0:T(8,128)(2,1)S(1)}, bf16[368,1152]{1,0:T(8,128)(2,1)}, u32[]{:S(2)}, u32[]{:S(2)}) collective-permute-start(bf16[368,1152]{1,0:T(8,128)(2,1)S(1)} %get-tuple-element.69), channel_id=1, source_target_pairs={{0,1},{1,0},{2,3},{3,2},{4,5},{5,4},{6,7},{7,6},{8,9},{9,8},{10,11... | collective-permute-start | bytes 2543624 | tf_op jit(solution)/shard_map/ppermute | solution.py:113
  18.7 575.3 %reduce-scatter.13.cloned.1.call-start = ((), (), s32[]{:S(2)}) async-start(), calls=%async_computation.9 | async-start | bytes 1566720
  18.9 74.1 %copy-start.72 = (pred[736]{0:T(1024)(128)(4,1)}, pred[736]{0:T(1024)(128)(4,1)S(1)}, u32[]{:S(2)}) copy-start(pred[736]{0:T(1024)(128)(4,1)S(1)} %fusion.180) | copy-start | bytes 2212
  73.8 53.5 %copy-start.11 = (bf16[736,576]{0,1:T(8,128)(2,1)}, bf16[736,576]{0,1:T(8,128)(2,1)S(1)}, u32[]{:S(2)}) copy-start(bf16[736,576]{0,1:T(8,128)(2,1)S(1)} %copy.62) | copy-start | bytes 2543620
  125.8 31.0 %collective-permute-start.1 = (bf16[368,1152]{1,0:T(8,128)(2,1)}, bf16[368,1152]{1,0:T(8,128)(2,1)}, u32[]{:S(2)}, u32[]{:S(2)}) collective-permute-start(bf16[368,1152]{1,0:T(8,128)(2,1)} %convolution_convert_fusion.10), channel_id=1, source_target_pairs={{0,1},{1,0},{2,3},{3,2},{4,5},{5,4},{6,7},{7,6},{8,9},{9,8},{10,11... | collective-permute-start | bytes 2543624 | tf_op jit(solution)/shard_map/ppermute | solution.py:113
  154.3 21.7 %copy-start.29 = (bf16[368,8,72]{0,2,1:T(8,128)(2,1)S(1)}, bf16[368,8,72]{0,2,1:T(8,128)(2,1)}, u32[]{:S(2)}) copy-start(bf16[368,8,72]{0,2,1:T(8,128)(2,1)} %get-tuple-element.80) | copy-start | bytes 1271812
  154.3 21.7 %copy-start.60 = (f32[1152]{0:T(1024)S(1)}, f32[1152]{0:T(1024)}, u32[]{:S(2)}) copy-start(f32[1152]{0:T(1024)} %get-tuple-element.50) | copy-start | bytes 13828
  155.3 20.7 %collective-permute-start.5 = (bf16[368,1152]{1,0:T(8,128)(2,1)S(1)}, bf16[368,1152]{1,0:T(8,128)(2,1)S(1)}, u32[]{:S(2)}, u32[]{:S(2)}) collective-permute-start(bf16[368,1152]{1,0:T(8,128)(2,1)S(1)} %convolution_convert_fusion.8), channel_id=1, source_target_pairs={{0,1},{1,0},{2,3},{3,2},{4,5},{5,4},{6,7},{7,6},{8,9},{9,8},{10,11... | collective-permute-start | bytes 2543624 | tf_op jit(solution)/shard_map/ppermute | solution.py:113
  181.2 22.1 %collective-permute-start.6 = (bf16[368,1152]{1,0:T(8,128)(2,1)}, bf16[368,1152]{1,0:T(8,128)(2,1)}, u32[]{:S(2)}, u32[]{:S(2)}) collective-permute-start(bf16[368,1152]{1,0:T(8,128)(2,1)} %get-tuple-element.94), channel_id=1, source_target_pairs={{0,1},{1,0},{2,3},{3,2},{4,5},{5,4},{6,7},{7,6},{8,9},{9,8},{10,11... | collective-permute-start | bytes 2543624 | tf_op jit(solution)/shard_map/ppermute | solution.py:113
  181.9 57.7 %copy-start.37 = (bf16[368,1152]{1,0:T(8,128)(2,1)}, bf16[368,1152]{1,0:T(8,128)(2,1)S(1)}, u32[]{:S(2)}) copy-start(bf16[368,1152]{1,0:T(8,128)(2,1)S(1)} %get-tuple-element.78) | copy-start | bytes 2543620
  181.9 87.4 %copy-start.35 = (bf16[368,1152]{1,0:T(8,128)(2,1)}, bf16[368,1152]{1,0:T(8,128)(2,1)S(1)}, u32[]{:S(2)}) copy-start(bf16[368,1152]{1,0:T(8,128)(2,1)S(1)} %get-tuple-element.77) | copy-start | bytes 2543620
  181.9 87.4 %collective-permute-start.8 = (bf16[368,1152]{1,0:T(8,128)(2,1)S(1)}, bf16[368,1152]{1,0:T(8,128)(2,1)}, u32[]{:S(2)}, u32[]{:S(2)}) collective-permute-start(bf16[368,1152]{1,0:T(8,128)(2,1)S(1)} %get-tuple-element.77), channel_id=1, source_target_pairs={{0,1},{1,0},{2,3},{3,2},{4,5},{5,4},{6,7},{7,6},{8,9},{9,8},{10,11... | collective-permute-start | bytes 2543624 | tf_op jit(solution)/shard_map/ppermute | solution.py:113
  183.4 56.2 %collective-permute-start.12 = (bf16[368,1152]{1,0:T(8,128)(2,1)S(1)}, bf16[368,1152]{1,0:T(8,128)(2,1)}, u32[]{:S(2)}, u32[]{:S(2)}) collective-permute-start(bf16[368,1152]{1,0:T(8,128)(2,1)S(1)} %get-tuple-element.78), channel_id=1, source_target_pairs={{0,1},{1,0},{2,3},{3,2},{4,5},{5,4},{6,7},{7,6},{8,9},{9,8},{10,11... | collective-permute-start | bytes 2543624 | tf_op jit(solution)/shard_map/ppermute | solution.py:113
  184.1 73.7 %collective-permute-start.2 = (bf16[368,1152]{1,0:T(8,128)(2,1)}, bf16[368,1152]{1,0:T(8,128)(2,1)}, u32[]{:S(2)}, u32[]{:S(2)}) collective-permute-start(bf16[368,1152]{1,0:T(8,128)(2,1)} %get-tuple-element.93), channel_id=1, source_target_pairs={{0,1},{1,0},{2,3},{3,2},{4,5},{5,4},{6,7},{7,6},{8,9},{9,8},{10,11... | collective-permute-start | bytes 2543624 | tf_op jit(solution)/shard_map/ppermute | solution.py:113
  250.7 31.3 %copy-start.24 = (bf16[736,2152]{1,0:T(8,128)(2,1)}, bf16[736,2152]{1,0:T(8,128)(2,1)S(1)}, u32[]{:S(2)}) copy-start(bf16[736,2152]{1,0:T(8,128)(2,1)S(1)} %fusion.27) | copy-start | bytes 9503236
  250.7 18.6 %slice-start = ((s8[5013504]{0:T(1024)(128)(4,1)}), s8[4194304]{0:T(1024)(128)(4,1)S(1)}, s32[]{:S(2)}) async-start(s8[5013504]{0:T(1024)(128)(4,1)} %bitcast.235), calls=%async_computation.12 | async-start | bytes 8388608
  253.1 28.9 %collective-permute-start.13 = (bf16[368,1152]{1,0:T(8,128)(2,1)S(1)}, bf16[368,1152]{1,0:T(8,128)(2,1)S(1)}, u32[]{:S(2)}, u32[]{:S(2)}) collective-permute-start(bf16[368,1152]{1,0:T(8,128)(2,1)S(1)} %convolution_convert_fusion.5), channel_id=1, source_target_pairs={{0,1},{1,0},{2,3},{3,2},{4,5},{5,4},{6,7},{7,6},{8,9},{9,8},{10,11... | collective-permute-start | bytes 2543624 | tf_op jit(solution)/shard_map/ppermute | solution.py:113
  279.0 19.6 %copy-start.25 = (bf16[736,2152]{1,0:T(8,128)(2,1)}, bf16[736,2152]{1,0:T(8,128)(2,1)S(1)}, u32[]{:S(2)}) copy-start(bf16[736,2152]{1,0:T(8,128)(2,1)S(1)} %fusion.21) | copy-start | bytes 9503236
  281.4 17.2 %copy-start.3 = (f32[368,1152]{1,0:T(8,128)S(1)}, f32[368,1152]{1,0:T(8,128)}, u32[]{:S(2)}) copy-start(f32[368,1152]{1,0:T(8,128)} %copy-done.2) | copy-start | bytes 5087236
  281.4 17.2 %collective-permute-start.9 = (bf16[368,1152]{1,0:T(8,128)(2,1)S(1)}, bf16[368,1152]{1,0:T(8,128)(2,1)S(1)}, u32[]{:S(2)}, u32[]{:S(2)}) collective-permute-start(bf16[368,1152]{1,0:T(8,128)(2,1)S(1)} %convolution_convert_fusion.6), channel_id=1, source_target_pairs={{0,1},{1,0},{2,3},{3,2},{4,5},{5,4},{6,7},{7,6},{8,9},{9,8},{10,11... | collective-permute-start | bytes 2543624 | tf_op jit(solution)/shard_map/ppermute | solution.py:113
  284.4 17.9 %copy-start.5 = (bf16[2,368,1152]{2,1,0:T(8,128)(2,1)S(1)}, bf16[2,368,1152]{2,1,0:T(8,128)(2,1)}, u32[]{:S(2)}) copy-start(bf16[2,368,1152]{2,1,0:T(8,128)(2,1)} %param.17) | copy-start | bytes 5087236
  304.5 37.2 %copy-start.32 = (bf16[8,72,736]{2,1,0:T(8,128)(2,1)S(1)}, bf16[8,72,736]{2,1,0:T(8,128)(2,1)}, u32[]{:S(2)}) copy-start(bf16[8,72,736]{2,1,0:T(8,128)(2,1)} %copy-done.31) | copy-start | bytes 2543620
  304.5 37.2 %copy-start.34 = (bf16[8,72,736]{2,1,0:T(8,128)(2,1)S(1)}, bf16[8,72,736]{2,1,0:T(8,128)(2,1)}, u32[]{:S(2)}) copy-start(bf16[8,72,736]{2,1,0:T(8,128)(2,1)} %copy-done.33) | copy-start | bytes 2543620
  305.8 35.0 %copy-start.40 = (bf16[368,1152]{1,0:T(8,128)(2,1)}, bf16[368,1152]{1,0:T(8,128)(2,1)S(1)}, u32[]{:S(2)}) copy-start(bf16[368,1152]{1,0:T(8,128)(2,1)S(1)} %convert_element_type.263) | copy-start | bytes 2543620
  306.3 34.5 %copy-start.42 = (bf16[368,1152]{1,0:T(8,128)(2,1)}, bf16[368,1152]{1,0:T(8,128)(2,1)S(1)}, u32[]{:S(2)}) copy-start(bf16[368,1152]{1,0:T(8,128)(2,1)S(1)} %convert_element_type.282) | copy-start | bytes 2543620
  306.3 21.9 %collective-permute-start.14 = (bf16[368,1152]{1,0:T(8,128)(2,1)S(1)}, bf16[368,1152]{1,0:T(8,128)(2,1)S(1)}, u32[]{:S(2)}, u32[]{:S(2)}) collective-permute-start(bf16[368,1152]{1,0:T(8,128)(2,1)S(1)} %convert_element_type.282), channel_id=1, source_target_pairs={{0,1},{1,0},{2,3},{3,2},{4,5},{5,4},{6,7},{7,6},{8,9},{9,8},{10,11... | collective-permute-start | bytes 2543624 | tf_op jit(solution)/shard_map/ppermute | solution.py:113
  307.2 33.5 %collective-permute-start.10 = (bf16[368,1152]{1,0:T(8,128)(2,1)S(1)}, bf16[368,1152]{1,0:T(8,128)(2,1)S(1)}, u32[]{:S(2)}, u32[]{:S(2)}) collective-permute-start(bf16[368,1152]{1,0:T(8,128)(2,1)S(1)} %convert_element_type.263), channel_id=1, source_target_pairs={{0,1},{1,0},{2,3},{3,2},{4,5},{5,4},{6,7},{7,6},{8,9},{9,8},{10,11... | collective-permute-start | bytes 2543624 | tf_op jit(solution)/shard_map/ppermute | solution.py:113
  346.4 249.2 %reduce-scatter.15.cloned.1.call-start = ((), (), s32[]{:S(2)}) async-start(), calls=%async_computation.10 | async-start | bytes 5326848
  360.8 236.7 %reduce-scatter.17.cloned.1.call-start = ((), (), s32[]{:S(2)}) async-start(), calls=%async_computation.11 | async-start | bytes 5326848
  363.2 109.5 %copy-start.46 = (f32[8,736]{1,0:T(8,128)}, f32[8,736]{1,0:T(8,128)S(1)}, u32[]{:S(2)}) copy-start(f32[8,736]{1,0:T(8,128)S(1)} %log_add_fusion.1) | copy-start | bytes 70660
  369.6 25.8 %collective-permute-start.7 = (bf16[368,1152]{1,0:T(8,128)(2,1)}, bf16[368,1152]{1,0:T(8,128)(2,1)}, u32[]{:S(2)}, u32[]{:S(2)}) collective-permute-start(bf16[368,1152]{1,0:T(8,128)(2,1)} %convolution_convert_fusion.7), channel_id=1, source_target_pairs={{0,1},{1,0},{2,3},{3,2},{4,5},{5,4},{6,7},{7,6},{8,9},{9,8},{10,11... | collective-permute-start | bytes 2543624 | tf_op jit(solution)/shard_map/ppermute | solution.py:113
  376.7 26.8 %collective-permute-start.3 = (bf16[368,1152]{1,0:T(8,128)(2,1)}, bf16[368,1152]{1,0:T(8,128)(2,1)}, u32[]{:S(2)}, u32[]{:S(2)}) collective-permute-start(bf16[368,1152]{1,0:T(8,128)(2,1)} %convolution_convert_fusion.9), channel_id=1, source_target_pairs={{0,1},{1,0},{2,3},{3,2},{4,5},{5,4},{6,7},{7,6},{8,9},{9,8},{10,11... | collective-permute-start | bytes 2543624 | tf_op jit(solution)/shard_map/ppermute | solution.py:113
  394.9 245.6 %reduce-scatter.11.cloned.1.call-start = ((), (), s32[]{:S(2)}) async-start(), calls=%async_computation.8 | async-start | bytes 4386816 | tf_op jit(solution)/shard_map/reduce_scatter | solution.py:137
  422.6 83.5 %copy-start.16 = (bf16[8,72,736]{2,1,0:T(8,128)(2,1)}, bf16[8,72,736]{2,1,0:T(8,128)(2,1)S(1)}, u32[]{:S(2)}) copy-start(bf16[8,72,736]{2,1,0:T(8,128)(2,1)S(1)} %fusion.161) | copy-start | bytes 2543620
  458.1 74.4 %collective-permute-start.15 = (bf16[368,1152]{1,0:T(8,128)(2,1)}, bf16[368,1152]{1,0:T(8,128)(2,1)}, u32[]{:S(2)}, u32[]{:S(2)}) collective-permute-start(bf16[368,1152]{1,0:T(8,128)(2,1)} %convolution_convert_fusion.3), channel_id=1, source_target_pairs={{0,1},{1,0},{2,3},{3,2},{4,5},{5,4},{6,7},{7,6},{8,9},{9,8},{10,11... | collective-permute-start | bytes 2543624 | tf_op jit(solution)/shard_map/ppermute | solution.py:113
  505.9 31.8 %collective-permute-start.11 = (bf16[368,1152]{1,0:T(8,128)(2,1)}, bf16[368,1152]{1,0:T(8,128)(2,1)}, u32[]{:S(2)}, u32[]{:S(2)}) collective-permute-start(bf16[368,1152]{1,0:T(8,128)(2,1)} %convolution_convert_fusion.4), channel_id=1, source_target_pairs={{0,1},{1,0},{2,3},{3,2},{4,5},{5,4},{6,7},{7,6},{8,9},{9,8},{10,11... | collective-permute-start | bytes 2543624 | tf_op jit(solution)/shard_map/ppermute | solution.py:113
  537.7 51.2 %copy-start.7 = (f32[368,1152]{1,0:T(8,128)S(1)}, f32[368,1152]{1,0:T(8,128)}, u32[]{:S(2)}) copy-start(f32[368,1152]{1,0:T(8,128)} %copy-done.6) | copy-start | bytes 5087236
  (62 other events, 370.5 us)
Sparse Core Ops, SparseCore 0:
  10.9 52.9 all-gather.4
  66.0 37.8 all-gather.6
  106.0 53.7 all-gather.8
  161.8 53.4 all-gather.10
  346.5 56.7 reduce-scatter.12
  407.2 76.9 reduce-scatter.14
  488.8 76.9 reduce-scatter.16
  569.7 70.7 reduce-scatter.10
where the time goes:
time: 655 us; the launch traced here: 650 us
  matrix products  251 us (38%)
  waiting for transfers between devices  204 us (31%)
  other arithmetic  85 us (13%)
  blocking collectives  40.5 us (6%)
  local copies, waits for them, and re-layouts  36.1 us (6%)
  starting transfers between devices  17.3 us (3%)
  between operations  15.7 us (2%)
    dot_general x28, matrix products, dot(): lax.dot_general(left, right, (dims, ((), ())), preferred_element_type=jnp...  163 us
    ppermute x16, waiting for transfers between devices, swap_halves(): return lax.ppermute(block, 'tp', [(0, 1), (1, 0)])  135 us
    reduce_scatter x1, waiting for transfers between devices, scatter_weight(): lax.psum_scatter(whole.astype(jnp.bfloat16), 'fsdp', scatter_dimension=0,...  41.2 us
    psum x1, blocking collectives, per_device(): total = lax.psum(jnp.concatenate(pieces), ('fsdp', 'tp'))  40.5 us
    convert_element_type x2, other arithmetic, attend_backward(): d_scores = (probs_full * (d_probs - row_inner)).astype(jnp.bfloat16)  25.9 us
    all_gather x4, waiting for transfers between devices, gather_weight(): return lax.all_gather(shard, 'fsdp', axis=0, tiled=True)  25.5 us
    dot_general x2, matrix products, attend_backward(): jnp.einsum('qhe,khe->hqk', grad_heads, value_heads, preferred_element_typ...  24 us
    dot_general x2, matrix products, attend_backward(): jnp.einsum('hqk,qhe->khe', probs_full.astype(jnp.bfloat16), grad_heads, p...  19.7 us
  transfers between devices with their start and end apart: 24, of which 11 were waited for; matrix products, arithmetic and copies ran while one was open for 54% of the time, Pallas kernels for 0%

commit v1 on v0

--- a/solution.py
+++ b/solution.py
@@ -240,7 +240,7 @@
         top_sums,
         unit_row,
     ]
-    total = lax.psum(jnp.concatenate(pieces), ("fsdp", "tp"))
+    total = jnp.sum(lax.all_gather(jnp.concatenate(pieces), ("fsdp", "tp")), axis=0)
     rows = total[: 8 * width].reshape(8, width)
     gain_total = jnp.stack([rows[0], rows[4]])
     bias_total = jnp.stack([rows[1], rows[2], rows[3], rows[6], rows[5], rows[7]])

time: 655 us -> 897 us (1.37)
  waiting for transfers between devices: 204 us -> 483 us
  blocking collectives: 40.5 us -> 0 us
    unnamed x11 -> x13, waiting for transfers between devices: 1.48 us -> 264 us
    psum x1 -> x0, blocking collectives: 40.5 us -> none  [per_device(): total = lax.psum(jnp.concatenate(pieces), ('fsdp', 'tp'))]
    reduce_scatter x1, waiting for transfers between devices: 41.2 us -> 73 us  [scatter_weight(): lax.psum_scatter(whole.astype(jnp.bfloat16), 'fsdp', scatter_dimension=0,...]
    ppermute x16, waiting for transfers between devices: 135 us -> 121 us  [swap_halves(): return lax.ppermute(block, 'tp', [(0, 1), (1, 0)])]
    reduce_sum x1, other arithmetic: 13.3 us -> 23.6 us  [per_device(): qkv_sums = jnp.sum(qkv_whole, axis=0, dtype=jnp.float32)]
  transfers between devices with their start and end apart: 24 -> 25, of which waited for: 11 -> 14; matrix products, arithmetic and copies ran while one was open for 54% -> 35% of each run, Pallas kernels for 0% -> 0%
where the time goes in v1:
time: 897 us; the launch traced here: 891 us
  waiting for transfers between devices  483 us (54%)
  matrix products  245 us (27%)
  other arithmetic  92.3 us (10%)
  local copies, waits for them, and re-layouts  37.3 us (4%)
  starting transfers between devices  17.7 us (2%)
  between operations  15.5 us (2%)
    unnamed x13, waiting for transfers between devices  264 us
    dot_general x28, matrix products, dot(): lax.dot_general(left, right, (dims, ((), ())), preferred_element_type=jnp...  158 us
    ppermute x16, waiting for transfers between devices, swap_halves(): return lax.ppermute(block, 'tp', [(0, 1), (1, 0)])  121 us
    reduce_scatter x1, waiting for transfers between devices, scatter_weight(): lax.psum_scatter(whole.astype(jnp.bfloat16), 'fsdp', scatter_dimension=0,...  73 us
    all_gather x4, waiting for transfers between devices, gather_weight(): return lax.all_gather(shard, 'fsdp', axis=0, tiled=True)  25.5 us
    convert_element_type x2, other arithmetic, attend_backward(): d_scores = (probs_full * (d_probs - row_inner)).astype(jnp.bfloat16)  25.1 us
    reduce_sum x1, other arithmetic, per_device(): qkv_sums = jnp.sum(qkv_whole, axis=0, dtype=jnp.float32)  23.6 us
    dot_general x2, matrix products, attend_backward(): jnp.einsum('qhe,khe->hqk', grad_heads, value_heads, preferred_element_typ...  23.6 us
  transfers between devices with their start and end apart: 25, of which 14 were waited for; matrix products, arithmetic and copies ran while one was open for 35% of the time, Pallas kernels for 0%

profile of v1, /device:TPU:0, one launch (start us, length us, event | category | flops | bytes accessed | tf_op | source)
XLA Modules:
  0.0 891.4 jit_solution(6095487101086427059)
XLA Ops:
  15.5 3.0 collective-permute-start.4
  18.9 19.4 %collective-permute-done.4 = bf16[368,1152]{1,0:T(8,128)(2,1)} collective-permute-done((bf16[368,1152]{1,0:T(8,128)(2,1)S(1)}, bf16[368,1152]{1,0:T(8,128)(2,1)}, u32[]{:S(2)}, u32[]{:S(2)}) %collective-permute-start.4) | collective-permute-done | bytes 847904 | tf_op jit(solution)/shard_map/ppermute | solution.py:113
  38.4 25.5 %all-gather.6.cloned.1.call-done = bf16[1152,1728]{1,0:T(8,128)(2,1)} async-done(((bf16[72,1728]{1,0:T(8,128)(2,1)}), bf16[1152,1728]{1,0:T(8,128)(2,1)}) %all-gather.6.cloned.1.call-update) | async-done | bytes 3981328 | tf_op jit(solution)/shard_map/all_gather | solution.py:133
  63.9 6.0 add_convert_fusion
  78.6 6.0 add_convert_fusion.1
  93.0 9.5 %fusion.204 = (f32[8,736]{1,0:T(8,128)S(1)}, f32[8,736,736]{1,2,0:T(8,128)}) fusion(bf16[736,8,72]{0,2,1:T(8,128)(2,1)} %bitcast.205, bf16[736,8,72]{0,2,1:T(8,128)(2,1)S(1)} %bitcast.195, pred[736]{0:T(1024)(128)(4,1)S(1)} %fusion.180), kind=kOutput, calls=%fused_computation.287 | convolution fusion | flops 637028608 | bytes 19054304 | tf_op jit(solution)/shard_map/qhe,khe->hqk/dot_general | solution.py:50
  102.5 8.8 fusion
  111.3 8.9 %fusion.157 = bf16[8,72,736]{2,1,0:T(8,128)(2,1)S(1)} fusion(bf16[736,8,72]{0,2,1:T(8,128)(2,1)S(1)} %bitcast.215, f32[8,736,736]{1,2,0:T(8,128)} %get-tuple-element.111, f32[8,736]{1,0:T(8,128)S(1)} %fusion, f32[8,736]{1,0:T(8,128)S(1)} %get-tuple-element.110), kind=kOutput, calls=%fused_computation.211 | convolution fusion | flops 637458432 | bytes 19077120 | tf_op jit(solution)/shard_map/hqk,khe->qhe/dot_general | solution.py:64
  122.3 3.4 convolution_convert_fusion.10
  127.3 9.2 %fusion.205 = (f32[8,736]{1,0:T(8,128)S(1)}, f32[8,736,736]{1,2,0:T(8,128)}) fusion(bf16[736,8,72]{0,2,1:T(8,128)(2,1)S(1)} %bitcast.207, bf16[736,8,72]{0,2,1:T(8,128)(2,1)S(1)} %bitcast.197, pred[736]{0:T(1024)(128)(4,1)} %copy-done.68), kind=kOutput, calls=%fused_computation.288 | convolution fusion | flops 637028608 | bytes 19054304 | tf_op jit(solution)/shard_map/qhe,khe->hqk/dot_general | solution.py:50
  136.5 8.8 fusion.1
  145.3 8.6 fusion.156
  156.7 19.3 %collective-permute-done.5 = bf16[368,1152]{1,0:T(8,128)(2,1)S(1)} collective-permute-done((bf16[368,1152]{1,0:T(8,128)(2,1)S(1)}, bf16[368,1152]{1,0:T(8,128)(2,1)S(1)}, u32[]{:S(2)}, u32[]{:S(2)}) %collective-permute-start.5) | collective-permute-done | bytes 847904 | tf_op jit(solution)/shard_map/ppermute | solution.py:113
  186.7 16.6 %collective-permute-done.6 = bf16[368,1152]{1,0:T(8,128)(2,1)} collective-permute-done((bf16[368,1152]{1,0:T(8,128)(2,1)}, bf16[368,1152]{1,0:T(8,128)(2,1)}, u32[]{:S(2)}, u32[]{:S(2)}) %collective-permute-start.6) | collective-permute-done | bytes 847904 | tf_op jit(solution)/shard_map/ppermute | solution.py:113
  203.4 10.3 %fusion.112 = f32[736,2152]{1,0:T(8,128)} fusion(bf16[1152,2152]{1,0:T(8,128)(2,1)} %all-gather.10.cloned.1.call-done, bf16[368,1152]{1,0:T(8,128)(2,1)} %collective-permute-done.6, bf16[368,1152]{1,0:T(8,128)(2,1)} %get-tuple-element.103), kind=kOutput, calls=%fused_computation.155 | convolution fusion | flops 3652632576 | bytes 12989440 | tf_op jit(solution)/shard_map/dot_general | solution.py:104
  213.7 26.0 %collective-permute-done.12 = bf16[368,1152]{1,0:T(8,128)(2,1)} collective-permute-done((bf16[368,1152]{1,0:T(8,128)(2,1)}, bf16[368,1152]{1,0:T(8,128)(2,1)}, u32[]{:S(2)}, u32[]{:S(2)}) %collective-permute-start.12) | collective-permute-done | bytes 847904 | tf_op jit(solution)/shard_map/ppermute | solution.py:113
  239.7 11.2 %fusion.27 = bf16[736,2152]{1,0:T(8,128)(2,1)S(1)} fusion(bf16[1152,2152]{1,0:T(8,128)(2,1)} %all-gather.12.cloned.1.call-done, f32[736,2152]{1,0:T(8,128)} %fusion.112, f32[2152]{0:T(1024)S(1)} %dynamic_slice.17, bf16[368,1152]{1,0:T(8,128)(2,1)} %collective-permute-done.12, bf16[368,1152]{1,0:T(8,128)(2,1)} %get-tuple-element.87), kind=kOutput, calls=%fused_computation.46 | convolution fusion | flops 3684310016 | bytes 16165792 | tf_op jit(solution)/shard_map/dot_general | solution.py:104
  254.1 3.8 collective-permute-done.2
  257.9 11.5 %multiply_convert_fusion.3 = (bf16[736,2152]{1,0:T(8,128)(2,1)}, bf16[736,2152]{1,0:T(8,128)(2,1)}, f32[736,2152]{1,0:T(8,128)}) fusion(f32[2152]{0:T(1024)S(1)} %dynamic_slice.17, f32[736,2152]{1,0:T(8,128)} %fusion.112, bf16[1152,2152]{1,0:T(8,128)(2,1)S(1)} %copy-done.73, bf16[368,1152]{1,0:T(8,128)(2,1)} %collective-permute-done.2, ...), kind=kOutput, calls=%fused_computation.52 | convolution fusion | flops 3684310016 | bytes 25669024 | tf_op jit(solution)/shard_map/dot_general | solution.py:104
  269.4 10.0 %fusion.21 = bf16[736,2152]{1,0:T(8,128)(2,1)S(1)} fusion(bf16[1152,2152]{1,0:T(8,128)(2,1)S(1)} %bitcast.236, f32[736,2152]{1,0:T(8,128)} %get-tuple-element.114, f32[2152]{0:T(1024)S(1)} %dynamic_slice.17, bf16[368,1152]{1,0:T(8,128)(2,1)} %collective-permute-done.8, bf16[368,1152]{1,0:T(8,128)(2,1)} %get-tuple-element.86), kind=kOutput, calls=%fused_computation.40 | convolution fusion | flops 3684310016 | bytes 16165792 | tf_op jit(solution)/shard_map/dot_general | solution.py:104
  285.0 14.2 %collective-permute-done.9 = bf16[368,1152]{1,0:T(8,128)(2,1)S(1)} collective-permute-done((bf16[368,1152]{1,0:T(8,128)(2,1)S(1)}, bf16[368,1152]{1,0:T(8,128)(2,1)S(1)}, u32[]{:S(2)}, u32[]{:S(2)}) %collective-permute-start.9) | collective-permute-done | bytes 847904 | tf_op jit(solution)/shard_map/ppermute | solution.py:113
  299.2 4.0 multiply_reduce_fusion.3
  303.2 3.1 fusion.194
  308.9 4.0 convert_reduce_fusion
  314.8 14.6 %collective-permute-done.14 = bf16[368,1152]{1,0:T(8,128)(2,1)} collective-permute-done((bf16[368,1152]{1,0:T(8,128)(2,1)}, bf16[368,1152]{1,0:T(8,128)(2,1)}, u32[]{:S(2)}, u32[]{:S(2)}) %collective-permute-start.14) | collective-permute-done | bytes 847904 | tf_op jit(solution)/shard_map/ppermute | solution.py:113
  329.5 2.8 fusion.164
  332.3 11.7 %multiply_reduce_fusion = (f32[8,736]{1,0:T(8,128)S(1)}, f32[8,736,736]{1,2,0:T(8,128)}) fusion(f32[8,736,736]{1,2,0:T(8,128)} %get-tuple-element.113, f32[8,736]{1,0:T(8,128)S(1)} %log_add_fusion, bf16[736,8,72]{0,2,1:T(8,128)(2,1)S(1)} %bitcast.219, bf16[736,8,72]{0,2,1:T(8,128)(2,1)S(1)} %bitcast.218), kind=kOutput, calls=%fused_computation.1 | convolution fusion | flops 637028608 | bytes 36411392 | tf_op jit(solution)/shard_map/qhe,khe->hqk/dot_general | solution.py:77
  344.0 12.6 %multiply_convert_fusion = bf16[8,736,736]{1,2,0:T(8,128)(2,1)S(1)} fusion(f32[8,736,736]{1,2,0:T(8,128)} %get-tuple-element.119, f32[8,736,736]{1,2,0:T(8,128)} %get-tuple-element.113, f32[8,736]{1,0:T(8,128)S(1)} %get-tuple-element.118, f32[8,736]{1,0:T(8,128)S(1)} %log_add_fusion), kind=kLoop, calls=%fused_computation | loop fusion | flops 17334272 | bytes 43382784 | tf_op jit(solution)/shard_map/convert_element_type | solution.py:81
  356.6 2.8 multiply_convert_fusion.4
  361.1 9.0 %fusion.161 = bf16[8,72,736]{2,1,0:T(8,128)(2,1)S(1)} fusion(bf16[736,8,72]{0,2,1:T(8,128)(2,1)S(1)} %bitcast.220, f32[8,736,736]{1,2,0:T(8,128)} %get-tuple-element.113, f32[8,736]{1,0:T(8,128)S(1)} %log_add_fusion), kind=kOutput, calls=%fused_computation.213 | convolution fusion | flops 633124864 | bytes 19053568 | tf_op jit(solution)/shard_map/hqk,qhe->khe/dot_general | solution.py:82
  371.6 9.0 %fusion.158 = bf16[8,72,736]{2,1,0:T(8,128)(2,1)S(1)} fusion(bf16[736,8,72]{0,2,1:T(8,128)(2,1)S(1)} %bitcast.221, f32[8,736,736]{1,2,0:T(8,128)} %get-tuple-element.111, f32[8,736]{1,0:T(8,128)S(1)} %log_add_fusion.1), kind=kOutput, calls=%fused_computation.212 | convolution fusion | flops 633124864 | bytes 19053568 | tf_op jit(solution)/shard_map/hqk,qhe->khe/dot_general | solution.py:82
  380.6 11.8 %multiply_reduce_fusion.1 = (f32[8,736]{1,0:T(8,128)S(1)}, f32[8,736,736]{1,2,0:T(8,128)}) fusion(f32[8,736,736]{1,2,0:T(8,128)} %get-tuple-element.111, f32[8,736]{1,0:T(8,128)S(1)} %log_add_fusion.1, bf16[736,8,72]{0,2,1:T(8,128)(2,1)S(1)} %bitcast.222, bf16[736,8,72]{0,2,1:T(8,128)(2,1)S(1)} %bitcast.216), kind=kOutput, calls=%fused_computation.4 | convolution fusion | flops 637028608 | bytes 36411392 | tf_op jit(solution)/shard_map/qhe,khe->hqk/dot_general | solution.py:77
  392.5 12.6 %multiply_convert_fusion.1 = bf16[8,736,736]{1,2,0:T(8,128)(2,1)S(1)} fusion(f32[8,736,736]{1,2,0:T(8,128)} %get-tuple-element.117, f32[8,736,736]{1,2,0:T(8,128)} %get-tuple-element.111, f32[8,736]{1,0:T(8,128)S(1)} %get-tuple-element.116, f32[8,736]{1,0:T(8,128)S(1)} %log_add_fusion.1), kind=kLoop, calls=%fused_computation.3 | loop fusion | flops 17334272 | bytes 43382784 | tf_op jit(solution)/shard_map/convert_element_type | solution.py:81
  419.0 23.6 %convert_reduce_fusion.1 = f32[1728]{0:T(1024)S(1)} fusion(bf16[736,576]{0,1:T(8,128)(2,1)S(1)} %bitcast.210, bf16[736,576]{0,1:T(8,128)(2,1)S(1)} %bitcast.200, bf16[736,576]{0,1:T(8,128)(2,1)S(1)} %bitcast.190, bf16[736,576]{0,1:T(8,128)(2,1)S(1)} %bitcast.213, bf16[736,576]{0,1:T(8,128)(2,1)S(1)} %bitcast.203, bf16[736,576]{0,1:T(8,128)(2,1)S(1)} %bitcast.193), kind=kLoop, calls=%fused_computation.19 | loop fusion | flops 33065280 | bytes 5094144 | tf_op jit(solution)/shard_map/reduce_sum | solution.py:215
  445.3 4.9 fusion.98
  453.4 7.1 fusion.60
  460.7 14.2 %convolution_convert_fusion.1 = bf16[1152,2152]{1,0:T(8,128)(2,1)} fusion(bf16[736,2152]{1,0:T(8,128)(2,1)} %copy-done.31, bf16[736,2152]{1,0:T(8,128)(2,1)} %copy-done.32, bf16[368,1152]{1,0:T(8,128)(2,1)} %collective-permute-done.6, bf16[368,1152]{1,0:T(8,128)(2,1)} %get-tuple-element.103, bf16[368,1152]{1,0:T(8,128)(2,1)} %collective-permute-done.2, ...), kind=kOutput, calls=%fused_computation.18 | convolution fusion | flops 7327198208 | bytes 14685184 | tf_op jit(solution)/shard_map/dot_general | solution.py:104
  475.0 14.2 %convolution_convert_fusion = bf16[1152,2152]{1,0:T(8,128)(2,1)} fusion(bf16[736,2152]{1,0:T(8,128)(2,1)} %get-tuple-element.105, bf16[736,2152]{1,0:T(8,128)(2,1)} %get-tuple-element.104, bf16[368,1152]{1,0:T(8,128)(2,1)} %collective-permute-done.12, bf16[368,1152]{1,0:T(8,128)(2,1)} %get-tuple-element.87, bf16[368,1152]{1,0:T(8,128)(2,1)} %collective-permute-done.8, ...), kind=kOutput, calls=%fused_computation.17 | convolution fusion | flops 7327198208 | bytes 14685184 | tf_op jit(solution)/shard_map/dot_general | solution.py:104
  489.6 6.3 convolution_convert_fusion.7
  496.6 12.7 %convolution_convert_fusion.2 = bf16[1152,1728]{1,0:T(8,128)(2,1)} fusion(bf16[368,1152]{1,0:T(8,128)(2,1)} %collective-permute-done.4, bf16[368,1152]{1,0:T(8,128)(2,1)} %copy-done.42, bf16[368,1152]{1,0:T(8,128)(2,1)} %collective-permute-done, bf16[368,1152]{1,0:T(8,128)(2,1)} %copy-done.41, bf16[736,576]{0,1:T(8,128)(2,1)} %bitcast.211, ...), kind=kOutput, calls=%fused_computation.30 | convolution fusion | flops 5906571264 | bytes 12460032 | tf_op jit(solution)/shard_map/dot_general | solution.py:104
  509.4 5.5 convolution_convert_fusion.9
  516.3 5.3 fusion.145
  521.7 6.5 collective-permute-done.3
  536.8 46.2 %all-reduce.6.cloned.1.call-done = f32[432640]{0:T(1024)} async-done(((f32[432640]{0:T(1024)}), f32[432640]{0:T(1024)}) %all-reduce.6.cloned.1.call-update) | async-done | bytes 1730576
  587.6 57.6 %reduce-scatter.13.cloned.1.call-done = bf16[72,576]{1,0:T(8,128)(2,1)} async-done(((bf16[1152,576]{1,0:T(8,128)(2,1)}), bf16[72,576]{1,0:T(8,128)(2,1)}) %reduce-scatter.13.cloned.1.call-update) | async-done | bytes 82960
  646.8 79.5 %reduce-scatter.15.cloned.1.call-done = bf16[72,2152]{1,0:T(8,128)(2,1)} async-done(((bf16[1152,2152]{1,0:T(8,128)(2,1)}), bf16[72,2152]{1,0:T(8,128)(2,1)}) %reduce-scatter.15.cloned.1.call-update) | async-done | bytes 309904
  728.1 79.6 %reduce-scatter.17.cloned.1.call-done = bf16[72,2152]{1,0:T(8,128)(2,1)} async-done(((bf16[1152,2152]{1,0:T(8,128)(2,1)}), bf16[72,2152]{1,0:T(8,128)(2,1)}) %reduce-scatter.17.cloned.1.call-update) | async-done | bytes 309904
  809.6 73.0 %reduce-scatter.11.cloned.1.call-done = bf16[72,1728]{1,0:T(8,128)(2,1)} async-done(((bf16[1152,1728]{1,0:T(8,128)(2,1)}), bf16[72,1728]{1,0:T(8,128)(2,1)}) %reduce-scatter.11.cloned.1.call-update) | async-done | bytes 248848 | tf_op jit(solution)/shard_map/reduce_scatter | solution.py:137
  (312 shorter events, 101.4 us)
Async XLA Ops:
  7.2 56.7 %all-gather.6.cloned.1.call-start = ((), (), s32[]{:S(2)}) async-start(), calls=%async_computation.4 | async-start | bytes 4386816 | tf_op jit(solution)/shard_map/all_gather | solution.py:133
  9.4 112.9 %all-gather.8.cloned.1.call-start = ((), (), s32[]{:S(2)}) async-start(), calls=%async_computation.5 | async-start | bytes 1566720 | tf_op jit(solution)/shard_map/all_gather | solution.py:133
  10.2 193.2 %all-gather.10.cloned.1.call-start = ((), (), s32[]{:S(2)}) async-start(), calls=%async_computation.6 | async-start | bytes 5326848 | tf_op jit(solution)/shard_map/all_gather | solution.py:133
  10.9 228.8 %all-gather.12.cloned.1.call-start = ((), (), s32[]{:S(2)}) async-start(), calls=%async_computation.7 | async-start | bytes 5326848 | tf_op jit(solution)/shard_map/all_gather | solution.py:133
  13.5 56.4 %copy-start.47 = (f32[368]{0:T(512)}, f32[368]{0:T(512)S(1)}, u32[]{:S(2)}) copy-start(f32[368]{0:T(512)S(1)} %get-tuple-element.123) | copy-start | bytes 4420
  13.5 56.4 %copy-start.49 = (f32[368]{0:T(512)}, f32[368]{0:T(512)S(1)}, u32[]{:S(2)}) copy-start(f32[368]{0:T(512)S(1)} %get-tuple-element.124) | copy-start | bytes 4420
  14.1 55.8 %copy-start.56 = (f32[368]{0:T(512)}, f32[368]{0:T(512)S(1)}, u32[]{:S(2)}) copy-start(f32[368]{0:T(512)S(1)} %add_rsqrt_fusion.3) | copy-start | bytes 4420
  14.2 55.8 %copy-start.59 = (f32[368]{0:T(512)}, f32[368]{0:T(512)S(1)}, u32[]{:S(2)}) copy-start(f32[368]{0:T(512)S(1)} %add_rsqrt_fusion.1) | copy-start | bytes 4420
  15.5 54.4 %copy-start.42 = (bf16[368,1152]{1,0:T(8,128)(2,1)}, bf16[368,1152]{1,0:T(8,128)(2,1)S(1)}, u32[]{:S(2)}) copy-start(bf16[368,1152]{1,0:T(8,128)(2,1)S(1)} %get-tuple-element.79) | copy-start | bytes 2543620
  15.5 63.0 %copy-start.41 = (bf16[368,1152]{1,0:T(8,128)(2,1)}, bf16[368,1152]{1,0:T(8,128)(2,1)S(1)}, u32[]{:S(2)}) copy-start(bf16[368,1152]{1,0:T(8,128)(2,1)S(1)} %get-tuple-element.78) | copy-start | bytes 2543620
  15.5 22.8 %collective-permute-start.4 = (bf16[368,1152]{1,0:T(8,128)(2,1)S(1)}, bf16[368,1152]{1,0:T(8,128)(2,1)}, u32[]{:S(2)}, u32[]{:S(2)}) collective-permute-start(bf16[368,1152]{1,0:T(8,128)(2,1)S(1)} %get-tuple-element.79), channel_id=1, source_target_pairs={{0,1},{1,0},{2,3},{3,2},{4,5},{5,4},{6,7},{7,6},{8,9},{9,8},{10,11... | collective-permute-start | bytes 2543624 | tf_op jit(solution)/shard_map/ppermute | solution.py:113
  18.6 60.0 %collective-permute-start = (bf16[368,1152]{1,0:T(8,128)(2,1)S(1)}, bf16[368,1152]{1,0:T(8,128)(2,1)}, u32[]{:S(2)}, u32[]{:S(2)}) collective-permute-start(bf16[368,1152]{1,0:T(8,128)(2,1)S(1)} %get-tuple-element.78), channel_id=1, source_target_pairs={{0,1},{1,0},{2,3},{3,2},{4,5},{5,4},{6,7},{7,6},{8,9},{9,8},{10,11... | collective-permute-start | bytes 2543624 | tf_op jit(solution)/shard_map/ppermute | solution.py:113
  18.7 564.3 %all-reduce.6.cloned.1.call-start = ((), (), s32[]{:S(2)}) async-start(), calls=%async_computation.9 | async-start | bytes 3465216
  18.9 74.0 %copy-start.68 = (pred[736]{0:T(1024)(128)(4,1)}, pred[736]{0:T(1024)(128)(4,1)S(1)}, u32[]{:S(2)}) copy-start(pred[736]{0:T(1024)(128)(4,1)S(1)} %fusion.180) | copy-start | bytes 2212
  73.8 53.5 %copy-start.14 = (bf16[736,576]{0,1:T(8,128)(2,1)}, bf16[736,576]{0,1:T(8,128)(2,1)S(1)}, u32[]{:S(2)}) copy-start(bf16[736,576]{0,1:T(8,128)(2,1)S(1)} %copy.78) | copy-start | bytes 2543620
  125.7 31.0 %collective-permute-start.1 = (bf16[368,1152]{1,0:T(8,128)(2,1)}, bf16[368,1152]{1,0:T(8,128)(2,1)}, u32[]{:S(2)}, u32[]{:S(2)}) collective-permute-start(bf16[368,1152]{1,0:T(8,128)(2,1)} %convolution_convert_fusion.10), channel_id=1, source_target_pairs={{0,1},{1,0},{2,3},{3,2},{4,5},{5,4},{6,7},{7,6},{8,9},{9,8},{10,11... | collective-permute-start | bytes 2543624 | tf_op jit(solution)/shard_map/ppermute | solution.py:113
  154.2 21.8 %copy-start.33 = (bf16[368,8,72]{0,2,1:T(8,128)(2,1)S(1)}, bf16[368,8,72]{0,2,1:T(8,128)(2,1)}, u32[]{:S(2)}) copy-start(bf16[368,8,72]{0,2,1:T(8,128)(2,1)} %get-tuple-element.89) | copy-start | bytes 1271812
  154.2 21.8 %copy-start.54 = (f32[1152]{0:T(1024)S(1)}, f32[1152]{0:T(1024)}, u32[]{:S(2)}) copy-start(f32[1152]{0:T(1024)} %get-tuple-element.59) | copy-start | bytes 13828
  155.2 20.8 %collective-permute-start.5 = (bf16[368,1152]{1,0:T(8,128)(2,1)S(1)}, bf16[368,1152]{1,0:T(8,128)(2,1)S(1)}, u32[]{:S(2)}, u32[]{:S(2)}) collective-permute-start(bf16[368,1152]{1,0:T(8,128)(2,1)S(1)} %convolution_convert_fusion.8), channel_id=1, source_target_pairs={{0,1},{1,0},{2,3},{3,2},{4,5},{5,4},{6,7},{7,6},{8,9},{9,8},{10,11... | collective-permute-start | bytes 2543624 | tf_op jit(solution)/shard_map/ppermute | solution.py:113
  178.7 124.5 %copy-start.2 = (f32[368,1152]{1,0:T(8,128)}, f32[368,1152]{1,0:T(8,128)S(1)}, u32[]{:S(2)}) copy-start(f32[368,1152]{1,0:T(8,128)S(1)} %get-tuple-element.69) | copy-start | bytes 5087236
  181.3 22.1 %collective-permute-start.6 = (bf16[368,1152]{1,0:T(8,128)(2,1)}, bf16[368,1152]{1,0:T(8,128)(2,1)}, u32[]{:S(2)}, u32[]{:S(2)}) collective-permute-start(bf16[368,1152]{1,0:T(8,128)(2,1)} %get-tuple-element.103), channel_id=1, source_target_pairs={{0,1},{1,0},{2,3},{3,2},{4,5},{5,4},{6,7},{7,6},{8,9},{9,8},{10,11... | collective-permute-start | bytes 2543624 | tf_op jit(solution)/shard_map/ppermute | solution.py:113
  183.1 86.3 %collective-permute-start.8 = (bf16[368,1152]{1,0:T(8,128)(2,1)}, bf16[368,1152]{1,0:T(8,128)(2,1)}, u32[]{:S(2)}, u32[]{:S(2)}) collective-permute-start(bf16[368,1152]{1,0:T(8,128)(2,1)} %get-tuple-element.86), channel_id=1, source_target_pairs={{0,1},{1,0},{2,3},{3,2},{4,5},{5,4},{6,7},{7,6},{8,9},{9,8},{10,11... | collective-permute-start | bytes 2543624 | tf_op jit(solution)/shard_map/ppermute | solution.py:113
  184.6 55.1 %collective-permute-start.12 = (bf16[368,1152]{1,0:T(8,128)(2,1)}, bf16[368,1152]{1,0:T(8,128)(2,1)}, u32[]{:S(2)}, u32[]{:S(2)}) collective-permute-start(bf16[368,1152]{1,0:T(8,128)(2,1)} %get-tuple-element.87), channel_id=1, source_target_pairs={{0,1},{1,0},{2,3},{3,2},{4,5},{5,4},{6,7},{7,6},{8,9},{9,8},{10,11... | collective-permute-start | bytes 2543624 | tf_op jit(solution)/shard_map/ppermute | solution.py:113
  185.2 72.6 %collective-permute-start.2 = (bf16[368,1152]{1,0:T(8,128)(2,1)}, bf16[368,1152]{1,0:T(8,128)(2,1)}, u32[]{:S(2)}, u32[]{:S(2)}) collective-permute-start(bf16[368,1152]{1,0:T(8,128)(2,1)} %get-tuple-element.102), channel_id=1, source_target_pairs={{0,1},{1,0},{2,3},{3,2},{4,5},{5,4},{6,7},{7,6},{8,9},{9,8},{10,11... | collective-permute-start | bytes 2543624 | tf_op jit(solution)/shard_map/ppermute | solution.py:113
  251.0 31.6 %copy-start.31 = (bf16[736,2152]{1,0:T(8,128)(2,1)}, bf16[736,2152]{1,0:T(8,128)(2,1)S(1)}, u32[]{:S(2)}) copy-start(bf16[736,2152]{1,0:T(8,128)(2,1)S(1)} %fusion.27) | copy-start | bytes 9503236
  251.0 18.4 %slice-start = ((s8[5013504]{0:T(1024)(128)(4,1)}), s8[4194304]{0:T(1024)(128)(4,1)S(1)}, s32[]{:S(2)}) async-start(s8[5013504]{0:T(1024)(128)(4,1)} %bitcast.235), calls=%async_computation.13 | async-start | bytes 8388608
  253.5 15.9 %slice-start.1 = ((s8[5013504]{0:T(1024)(128)(4,1)}), s8[819200]{0:T(1024)(128)(4,1)S(1)}, s32[]{:S(2)}) async-start(s8[5013504]{0:T(1024)(128)(4,1)} %bitcast.235), calls=%async_computation.14 | async-start | bytes 1638400
  253.5 29.0 %collective-permute-start.13 = (bf16[368,1152]{1,0:T(8,128)(2,1)S(1)}, bf16[368,1152]{1,0:T(8,128)(2,1)S(1)}, u32[]{:S(2)}, u32[]{:S(2)}) collective-permute-start(bf16[368,1152]{1,0:T(8,128)(2,1)S(1)} %convolution_convert_fusion.5), channel_id=1, source_target_pairs={{0,1},{1,0},{2,3},{3,2},{4,5},{5,4},{6,7},{7,6},{8,9},{9,8},{10,11... | collective-permute-start | bytes 2543624 | tf_op jit(solution)/shard_map/ppermute | solution.py:113
  279.4 19.8 %copy-start.32 = (bf16[736,2152]{1,0:T(8,128)(2,1)}, bf16[736,2152]{1,0:T(8,128)(2,1)S(1)}, u32[]{:S(2)}) copy-start(bf16[736,2152]{1,0:T(8,128)(2,1)S(1)} %fusion.21) | copy-start | bytes 9503236
  281.9 17.3 %copy-start.5 = (f32[368,1152]{1,0:T(8,128)S(1)}, f32[368,1152]{1,0:T(8,128)}, u32[]{:S(2)}) copy-start(f32[368,1152]{1,0:T(8,128)} %copy-done.4) | copy-start | bytes 5087236
  281.9 17.3 %collective-permute-start.9 = (bf16[368,1152]{1,0:T(8,128)(2,1)S(1)}, bf16[368,1152]{1,0:T(8,128)(2,1)S(1)}, u32[]{:S(2)}, u32[]{:S(2)}) collective-permute-start(bf16[368,1152]{1,0:T(8,128)(2,1)S(1)} %convolution_convert_fusion.6), channel_id=1, source_target_pairs={{0,1},{1,0},{2,3},{3,2},{4,5},{5,4},{6,7},{7,6},{8,9},{9,8},{10,11... | collective-permute-start | bytes 2543624 | tf_op jit(solution)/shard_map/ppermute | solution.py:113
  307.3 22.1 %collective-permute-start.14 = (bf16[368,1152]{1,0:T(8,128)(2,1)}, bf16[368,1152]{1,0:T(8,128)(2,1)}, u32[]{:S(2)}, u32[]{:S(2)}) collective-permute-start(bf16[368,1152]{1,0:T(8,128)(2,1)} %convert_element_type.282), channel_id=1, source_target_pairs={{0,1},{1,0},{2,3},{3,2},{4,5},{5,4},{6,7},{7,6},{8,9},{9,8},{10,11... | collective-permute-start | bytes 2543624 | tf_op jit(solution)/shard_map/ppermute | solution.py:113
  308.9 20.5 %copy-start.25 = (bf16[1152,576]{1,0:T(8,128)(2,1)S(1)}, bf16[1152,576]{1,0:T(8,128)(2,1)}, u32[]{:S(2)}) copy-start(bf16[1152,576]{1,0:T(8,128)(2,1)} %all-gather.8.cloned.1.call-done) | copy-start | bytes 3981316
  313.4 56.7 %copy-start.40 = (bf16[368,1152]{1,0:T(8,128)(2,1)}, bf16[368,1152]{1,0:T(8,128)(2,1)S(1)}, u32[]{:S(2)}) copy-start(bf16[368,1152]{1,0:T(8,128)(2,1)S(1)} %convert_element_type.263) | copy-start | bytes 2543620
  313.4 18.8 %copy-start.30 = (bf16[736,576]{0,1:T(8,128)(2,1)S(1)}, bf16[736,576]{0,1:T(8,128)(2,1)}, u32[]{:S(2)}) copy-start(bf16[736,576]{0,1:T(8,128)(2,1)} %copy.76) | copy-start | bytes 2543620
  313.4 56.7 %collective-permute-start.10 = (bf16[368,1152]{1,0:T(8,128)(2,1)S(1)}, bf16[368,1152]{1,0:T(8,128)(2,1)S(1)}, u32[]{:S(2)}, u32[]{:S(2)}) collective-permute-start(bf16[368,1152]{1,0:T(8,128)(2,1)S(1)} %convert_element_type.263), channel_id=1, source_target_pairs={{0,1},{1,0},{2,3},{3,2},{4,5},{5,4},{6,7},{7,6},{8,9},{9,8},{10,11... | collective-permute-start | bytes 2543624 | tf_op jit(solution)/shard_map/ppermute | solution.py:113
  359.4 59.7 %copy-start.16 = (bf16[8,72,736]{2,1,0:T(8,128)(2,1)}, bf16[8,72,736]{2,1,0:T(8,128)(2,1)S(1)}, u32[]{:S(2)}) copy-start(bf16[8,72,736]{2,1,0:T(8,128)(2,1)S(1)} %multiply_convert_fusion.4) | copy-start | bytes 2543620
  370.1 48.9 %copy-start.22 = (bf16[8,72,736]{2,1,0:T(8,128)(2,1)}, bf16[8,72,736]{2,1,0:T(8,128)(2,1)S(1)}, u32[]{:S(2)}) copy-start(bf16[8,72,736]{2,1,0:T(8,128)(2,1)S(1)} %fusion.161) | copy-start | bytes 2543620
  380.6 38.4 %copy-start.23 = (bf16[8,72,736]{2,1,0:T(8,128)(2,1)}, bf16[8,72,736]{2,1,0:T(8,128)(2,1)S(1)}, u32[]{:S(2)}) copy-start(bf16[8,72,736]{2,1,0:T(8,128)(2,1)S(1)} %fusion.158) | copy-start | bytes 2543620
  414.1 28.9 %collective-permute-start.15 = (bf16[368,1152]{1,0:T(8,128)(2,1)S(1)}, bf16[368,1152]{1,0:T(8,128)(2,1)S(1)}, u32[]{:S(2)}, u32[]{:S(2)}) collective-permute-start(bf16[368,1152]{1,0:T(8,128)(2,1)S(1)} %convolution_convert_fusion.3), channel_id=1, source_target_pairs={{0,1},{1,0},{2,3},{3,2},{4,5},{5,4},{6,7},{7,6},{8,9},{9,8},{10,11... | collective-permute-start | bytes 2543624 | tf_op jit(solution)/shard_map/ppermute | solution.py:113
  417.6 27.6 %collective-permute-start.11 = (bf16[368,1152]{1,0:T(8,128)(2,1)S(1)}, bf16[368,1152]{1,0:T(8,128)(2,1)S(1)}, u32[]{:S(2)}, u32[]{:S(2)}) collective-permute-start(bf16[368,1152]{1,0:T(8,128)(2,1)S(1)} %convolution_convert_fusion.4), channel_id=1, source_target_pairs={{0,1},{1,0},{2,3},{3,2},{4,5},{5,4},{6,7},{7,6},{8,9},{9,8},{10,11... | collective-permute-start | bytes 2543624 | tf_op jit(solution)/shard_map/ppermute | solution.py:113
  453.3 191.9 %reduce-scatter.13.cloned.1.call-start = ((), (), s32[]{:S(2)}) async-start(), calls=%async_computation.10 | async-start | bytes 1566720
  460.5 265.8 %reduce-scatter.15.cloned.1.call-start = ((), (), s32[]{:S(2)}) async-start(), calls=%async_computation.11 | async-start | bytes 5326848
  474.9 332.8 %reduce-scatter.17.cloned.1.call-start = ((), (), s32[]{:S(2)}) async-start(), calls=%async_computation.12 | async-start | bytes 5326848
  489.2 393.4 %reduce-scatter.11.cloned.1.call-start = ((), (), s32[]{:S(2)}) async-start(), calls=%async_computation.8 | async-start | bytes 4386816 | tf_op jit(solution)/shard_map/reduce_scatter | solution.py:137
  495.9 20.3 %collective-permute-start.7 = (bf16[368,1152]{1,0:T(8,128)(2,1)}, bf16[368,1152]{1,0:T(8,128)(2,1)}, u32[]{:S(2)}, u32[]{:S(2)}) collective-permute-start(bf16[368,1152]{1,0:T(8,128)(2,1)} %convolution_convert_fusion.7), channel_id=1, source_target_pairs={{0,1},{1,0},{2,3},{3,2},{4,5},{5,4},{6,7},{7,6},{8,9},{9,8},{10,11... | collective-permute-start | bytes 2543624 | tf_op jit(solution)/shard_map/ppermute | solution.py:113
  509.4 18.8 %slice-start.2 = ((s8[5013504]{0:T(1024)(128)(4,1)}), s8[4194304]{0:T(1024)(128)(4,1)S(1)}, s32[]{:S(2)}) async-start(s8[5013504]{0:T(1024)(128)(4,1)} %bitcast.237), calls=%async_computation.15 | async-start | bytes 8388608
  514.9 13.4 %collective-permute-start.3 = (bf16[368,1152]{1,0:T(8,128)(2,1)S(1)}, bf16[368,1152]{1,0:T(8,128)(2,1)S(1)}, u32[]{:S(2)}, u32[]{:S(2)}) collective-permute-start(bf16[368,1152]{1,0:T(8,128)(2,1)S(1)} %convolution_convert_fusion.9), channel_id=1, source_target_pairs={{0,1},{1,0},{2,3},{3,2},{4,5},{5,4},{6,7},{7,6},{8,9},{9,8},{10,11... | collective-permute-start | bytes 2543624 | tf_op jit(solution)/shard_map/ppermute | solution.py:113
  (59 other events, 331.5 us)
Sparse Core Ops, SparseCore 0:
  10.9 52.9 all-gather.5
  66.0 37.8 all-gather.7
  106.0 53.6 all-gather.9
  161.7 53.5 all-gather.11
  453.4 129.5 all-reduce.5
  586.6 58.5 reduce-scatter.12
  649.2 76.9 reduce-scatter.14
  730.8 76.8 reduce-scatter.16
  811.7 70.8 reduce-scatter.10
